TPU v7x, 32 devices: a whole 2x2x4 slice. The times are simulated.
32 devices in a mesh: leaf: 8 (over z, y), front: 4 (over x, core).
Axes of the slice: x: 2, y: 2, z: 4, core: 2. Of those that a mesh axis runs over, the one named last changes fastest.
Arguments:
- leaf_fronts: float32 [8, 1024, 1024], P('leaf', 'front')
- coupling_cols: int32 [8, 4, 224, 128], P('leaf', 'front'), may hold values from 0 to 1023, as said below
- coupling_vals: float32 [8, 4, 224, 128], P('leaf', 'front'), may hold values from -0.1 to 0.1
- sep_diag: float32 [8, 4, 224], P('leaf', 'front'), may hold values from 1 to 3
- child_maps: int32 [14, 512], replicated, may hold values from 0 to 1023, as said below
Outputs:
- factors: float32 [8, 4, 480, 512], P('leaf', 'front')
- log_det: float32 [], replicated
Inputs may be any that keep to these rules, and one draw needn't show every extreme that they name: `coupling_cols`: each coupling column is at most the index, in its front, of the row that holds it, so every entry lies on or below the diagonal. `child_maps`: the 512 entries of each row are distinct.
All inputs are finite; a program needn't handle non-finite values.
Results may differ from a plain program's by a relative error of at most 0.0001.
Values sent between devices are 32-bit elements; how exact they have to be, the bound alone decides.
No kernel may reach another device: no remote copies, remote signals or barrier semaphores. Data moves between devices by JAX's collectives and lax.ppermute only.
A program may use at most 128 MiB of HBM per device.

v0:
```python
import functools

import jax
import jax.numpy as jnp
from jax import lax
from jax.experimental import pallas as pl
from jax.experimental.pallas import tpu as pltpu
from jax.sharding import Mesh, PartitionSpec as P

SEP = 512
BND = 512
WIDTH = SEP + BND
KC = 128
T = 128
NB = SEP // T
PANEL = 32
PIECES = 3
STEP = 32
TILE = 256
NPACK = NB * (NB + 1) // 2
F32 = jnp.float32
BF16 = jnp.bfloat16
VMEM_LIMIT = 28 * 1024 * 1024


def pack_index(i, j):
    return i * (i + 1) // 2 + j


def split(x):
    hi = x.astype(BF16)
    return hi, (x - hi.astype(F32)).astype(BF16)


def dot_nt(a, b):
    return lax.dot_general(a, b, (((1,), (1,)), ((), ())), preferred_element_type=F32)


def dot_nn(a, b):
    return lax.dot_general(a, b, (((1,), (0,)), ((), ())), preferred_element_type=F32)


def mm_nt(a, b):
    a_hi, a_lo = split(a)
    b_hi, b_lo = split(b)
    return dot_nt(a_hi, b_hi) + (dot_nt(a_hi, b_lo) + dot_nt(a_lo, b_hi))


def iota2(shape, dim):
    return lax.broadcasted_iota(jnp.int32, shape, dim)


def tri_sym(block):
    n = block.shape[0]
    rows, cols = iota2((n, n), 0), iota2((n, n), 1)
    low = jnp.where(cols <= rows, block, 0.0)
    strict = jnp.where(cols < rows, block, 0.0)
    return low + strict.T


def row_of(x, k):
    return jnp.broadcast_to(x[k : k + 1], (8, T))


def lane_of(x, k):
    return jnp.broadcast_to(x[:, k : k + 1], (8, T))


def tree_sum(terms):
    while len(terms) > 1:
        terms = [sum(terms[i : i + 2][1:], terms[i]) for i in range(0, len(terms), 2)]
    return terms[0]


def reciprocal(x):
    return pl.reciprocal(x, approx=True)


def eliminate_eight(groups, s, c, keep, lane, sub, tmp_ref):
    panel = groups[s]
    inside = (lane >= c) & (lane < c + 8)
    base = c * 9
    for m in range(8):
        tmp_ref[base + 8 * m : base + 8 * m + 8, :] = lane_of(panel, c + m)
    tmp_ref[base + 64 : base + 72, :] = jnp.where(inside, jnp.where(lane - c == sub, 1.0, 0.0), panel)

    def row(n):
        return jnp.broadcast_to(tmp_ref[base + n : base + n + 1, :], (8, T))

    d = {(i, m): row(8 * m + i) for m in range(8) for i in range(m + 1)}
    rows = [row(64 + k) for k in range(8)]
    upper_acc = jnp.zeros((8, T), F32)
    inv_acc = jnp.zeros((8, T), F32)
    to_p, to_q, first = {}, {}, {}

    def emit(k, line, entries, root):
        inv_row = line * root
        for m in range(k, 8):
            line = jnp.where(lane == c + m, entries[m], line)
        return jnp.where(sub == k, line * root, upper_acc), jnp.where(sub == k, inv_row, inv_acc)

    for p in range(0, 8, 2):
        q = p + 1
        a, b, e = d[p, p], d[p, q], d[q, q]
        det = a * e - b * b
        recip = reciprocal(det)
        rest = range(q + 1, 8)
        w = {i: e * d[p, i] - b * d[q, i] for i in rest}
        z = {i: a * d[q, i] - b * d[p, i] for i in rest}
        root_p = lax.rsqrt(a)
        inv_a = root_p * root_p
        ratio = b * inv_a
        schur = det * inv_a
        upper_acc, inv_acc = emit(p, rows[p], {m: d[p, m] for m in range(p, 8)}, root_p)
        line_q = {m: d[q, m] - ratio * d[p, m] for m in rest}
        line_q[q] = schur
        upper_acc, inv_acc = emit(q, rows[q] - ratio * rows[p], line_q, lax.rsqrt(schur))
        for i in rest:
            for m in range(i, 8):
                d[i, m] = d[i, m] - (w[i] * d[p, m] + z[i] * d[q, m]) * recip
        for i in rest:
            to_p[p, i], to_q[p, i] = w[i] * recip, z[i] * recip
            rows[i] = rows[i] - (to_p[p, i] * rows[p] + to_q[p, i] * rows[q])
        first[p] = (e * rows[p] - b * rows[q]) * recip
        first[q] = (a * rows[q] - b * rows[p]) * recip
    if s + 1 < keep:
        sol = [None] * 8
        for p in (6, 4, 2, 0):
            rest = range(p + 2, 8)
            sol[p], sol[p + 1] = first[p], first[p + 1]
            if p < 6:
                sol[p] = sol[p] - tree_sum([to_p[p, m] * sol[m] for m in rest])
                sol[p + 1] = sol[p + 1] - tree_sum([to_q[p, m] * sol[m] for m in rest])
        for g in range(s + 1, keep):
            old = groups[g]
            groups[g] = jnp.where(inside, 0.0, old) - tree_sum([lane_of(old, c + k) * sol[k] for k in range(8)])
    return jnp.where(lane >= c + sub, upper_acc, 0.0), jnp.where(lane <= c + sub, inv_acc, 0.0)


def chol_and_inverse(sym, tmp_ref):
    lane, sub = iota2((8, T), 1), iota2((8, T), 0)
    per = PANEL // 8
    diag = jnp.sum(jnp.where(iota2((T, T), 0) == iota2((T, T), 1), sym, 0.0), axis=0, keepdims=True)
    scale = jnp.broadcast_to(lax.rsqrt(diag), (T, T))
    sym = (sym * scale) * scale.T
    groups = [sym[8 * g : 8 * g + 8] for g in range(T // 8)]
    upper_rows, inv_rows = [], []
    for p in range(T // PANEL):
        for s in range(p * per, (p + 1) * per):
            upper, inv = eliminate_eight(groups, s, 8 * s, (p + 1) * per, lane, sub, tmp_ref)
            upper_rows.append(upper)
            inv_rows.append(inv)
        end = (p + 1) * PANEL
        if end < T:
            both = jnp.concatenate(
                [jnp.where(lane < end, inv_rows[s], upper_rows[s]) for s in range(p * per, (p + 1) * per)], axis=0
            )
            hi, lo = split(both)
            product = lax.dot_general(
                jnp.concatenate([hi, lo, hi], axis=0), jnp.concatenate([hi, hi, lo], axis=0),
                (((0,), (0,)), ((), ())), preferred_element_type=F32,
            )
            done = (lane >= p * PANEL) & (lane < end)
            for g in range((p + 1) * per, T // 8):
                groups[g] = jnp.where(done, 0.0, groups[g]) - product[8 * g : 8 * g + 8]
    return jnp.concatenate(upper_rows, axis=0) * (diag * scale[0:1]), jnp.concatenate(inv_rows, axis=0) * scale


def factor_panel(f_ref, x_ref, log_ref, tmp_ref, rows, blocks):
    width = blocks * T
    log_ref[...] = jnp.zeros_like(log_ref)

    @pl.loop(0, blocks)
    def _(j):
        at = pl.multiple_of(j * T, T)
        upper, inv = chol_and_inverse(tri_sym(f_ref[pl.ds(at, T), pl.ds(at, T)]), tmp_ref)
        f_ref[pl.ds(at, T), pl.ds(at, T)] = upper.T
        x_ref[pl.ds(at, T), :] = inv
        eye = iota2((T, T), 0) == iota2((T, T), 1)
        diag = jnp.sum(jnp.where(eye, upper, 0.0), axis=0, keepdims=True)
        log_ref[0:1, :] += jnp.log(diag)
        for k in range(blocks):
            first = (k + 1) * T
            if first >= rows:
                continue

            @pl.when(j == k)
            def _():
                below = mm_nt(f_ref[first:rows, k * T : first], inv)
                f_ref[first:rows, k * T : first] = below
                if first < width:
                    f_ref[first:rows, first:width] -= mm_nt(below, below[: width - first])


def zero_above(f_ref, blocks):
    for i in range(blocks - 1):
        f_ref[i * T : (i + 1) * T, (i + 1) * T : blocks * T] = jnp.zeros((T, (blocks - 1 - i) * T), F32)


def log_total(log_ref):
    return 2.0 * jnp.sum(log_ref[0:1, :], axis=1, keepdims=True)


def write_own(out_ref, f_ref, start):
    size = out_ref.shape[0]
    if size % 8 == 0:
        out_ref[...] = f_ref[pl.ds(pl.multiple_of(start, 8), size), 0:SEP]
    else:
        base = pl.multiple_of(start // 8 * 8, 8)
        block = f_ref[pl.ds(base, 8), 0:SEP]
        offset = start - base
        piece = block[0:size]
        for shift in range(size, 8, size):
            piece = jnp.where(offset == shift, block[shift : shift + size], piece)
        out_ref[...] = piece


def write_update(pk_ref, below, tail_of, log_value):
    hi, lo = split(below)
    rows, cols = iota2((T, T), 0), iota2((T, T), 1)
    for i in range(NB):
        here = slice(i * T, (i + 1) * T)
        upto = slice(0, (i + 1) * T)
        prod = dot_nt(hi[here], hi[upto]) + (dot_nt(hi[here], lo[upto]) + dot_nt(lo[here], hi[upto]))
        for j in range(i + 1):
            block = tail_of(i, j) - prod[:, j * T : (j + 1) * T]
            if i == 0:
                block = jnp.where((rows == 0) & (cols == T - 1), log_value, block)
            pk_ref[pack_index(i, j)] = block


def place(pieces, work, front, want_tail):
    count = len(pieces)
    half = count // 2
    size = pieces[0].shape[0]
    for m, piece in enumerate(pieces):
        source = front ^ m

        @pl.when((source >= half) == want_tail)
        def _():
            at = pl.multiple_of((source & (half - 1)) * size, 8)
            work[pl.ds(at, size), :] = piece[...]


def head_kernel(n, pos_ref, *refs):
    pieces, (fac_ref, x_ref, log_ref, tmp_ref) = refs[:n], refs[n:]
    place(pieces, fac_ref, pos_ref[1], False)
    factor_panel(fac_ref, x_ref, log_ref, tmp_ref, SEP, NB)
    zero_above(fac_ref, NB)


def below_kernel(n, pos_ref, fac, inv, *refs):
    pieces, (own_ref, below_ref, stack) = refs[:n], refs[n:]
    front = pos_ref[1]
    place(pieces, below_ref, front, True)
    for j in range(NB):
        here = slice(j * T, (j + 1) * T)
        solved = mm_nt(below_ref[:, here], inv[here, :])
        below_ref[:, here] = solved
        if j + 1 < NB:
            rest = slice((j + 1) * T, SEP)
            below_ref[:, rest] -= mm_nt(solved, fac[rest, here])
    stack[0:SEP, :] = fac[...]
    stack[SEP:, :] = below_ref[...]
    write_own(own_ref, stack, front * own_ref.shape[0])


def update_kernel(n, pos_ref, below_ref, log_ref, *refs):
    pieces, (pk_ref, tail_ref) = refs[:n], refs[n:]
    place(pieces, tail_ref, pos_ref[1], True)

    def tail_of(i, j):
        return tail_ref[i * T : (i + 1) * T, j * T : (j + 1) * T]

    write_update(pk_ref, below_ref[...], tail_of, log_total(log_ref))


def expand(pk_ref, u_hi, u_lo):
    rows, cols = iota2((T, T), 0), iota2((T, T), 1)
    for i in range(NB):
        for j in range(i + 1):
            block = pk_ref[pack_index(i, j)]
            if i == j:
                low = jnp.where(cols <= rows, block, 0.0)
                block = low + jnp.where(cols < rows, block, 0.0).T
            hi, lo = split(block)
            u_hi[i * T : (i + 1) * T, j * T : (j + 1) * T] = hi
            u_lo[i * T : (i + 1) * T, j * T : (j + 1) * T] = lo
            if i != j:
                hi, lo = split(block.T)
                u_hi[j * T : (j + 1) * T, i * T : (i + 1) * T] = hi
                u_lo[j * T : (j + 1) * T, i * T : (i + 1) * T] = lo


def extend_add(pk_ref, index_row, emit, last, u_hi, u_lo, hot, y_hi, y_lo):
    expand(pk_ref, u_hi, u_lo)

    @pl.loop(0, WIDTH // TILE)
    def _(tile):
        at = pl.multiple_of(tile * TILE, TILE)
        ids = iota2((TILE, BND), 0) + at
        match = jnp.where(ids == index_row, 1.0, 0.0).astype(BF16)
        hot[pl.ds(at, TILE), :] = match
        y_hi[pl.ds(at, TILE), :] = dot_nn(match, u_hi[...]).astype(BF16)
        y_lo[pl.ds(at, TILE), :] = dot_nn(match, u_lo[...]).astype(BF16)

    for a in range(WIDTH // TILE):
        here = slice(a * TILE, (a + 1) * TILE)
        for b in range(a + 1):
            if last and b * TILE >= SEP:
                continue
            there = slice(b * TILE, (b + 1) * TILE)
            part = dot_nt(y_hi[here, :], hot[there, :]) + dot_nt(y_lo[here, :], hot[there, :])
            emit(a, b, part)


def map_row(level, n_leaf, pos_ref, maps_ref, sibling):
    base = 2 * n_leaf - 2 * (n_leaf >> (level - 1))
    own = pos_ref[0] >> (level - 1)
    number = base + (own ^ 1 if sibling else own)
    return maps_ref[pl.ds(number, 1), :]


def owned_blocks(core, last):
    rows = [2 * turn + (turn + core) % 2 for turn in range(WIDTH // T // 2)]
    return [(i, j) for i in rows for j in range(min(i + 1, NB if last else 2 * NB))]


def piece_bounds(last):
    total = len(owned_blocks(0, last))
    return [total * n // PIECES for n in range(PIECES + 1)]


def coupling_kernel(last, pos_ref, lists_ref, *refs):
    out_refs, (dense, totals) = refs[:-2], refs[-2:]
    bounds = piece_bounds(last)
    core = pos_ref[1] & 1
    size = lists_ref.shape[1] - 8
    eye = iota2((T, T), 0) == iota2((T, T), 1)
    limit = NB if last else 2 * NB
    steps = WIDTH // 2 // STEP

    @pl.loop(0, steps + 1)
    def _(step):
        spread_rows(totals, dense, jnp.maximum(step - 1, 0) * STEP)
        gather_rows(lists_ref, totals, jnp.minimum(step, steps - 1) * STEP, core)

    def turn_of(turn, offset):
        i = 2 * turn + ((turn + core) & 1)
        diag = jnp.zeros((1, T), F32)
        for n in range(max(1, T // size)):
            diag = diag + lists_ref[i * T // size + n, size : size + 1, 0:T]
        for j in range(limit):
            for first, end, out_ref in zip(bounds, bounds[1:], out_refs):

                @pl.when((j <= i) & (offset + j >= first) & (offset + j < end))
                def _():
                    block = dense[pl.ds(pl.multiple_of(turn * WIDTH + j * T, T), T), :]
                    out_ref[offset + j - first] = block + jnp.where(eye & (j == i), diag, 0.0)

        return offset + jnp.minimum(i + 1, limit)

    lax.fori_loop(0, WIDTH // T // 2, turn_of, 0)


def own_kernel(level, n_leaf, last, pos_ref, pk_ref, maps_ref, f_ref, u_hi, u_lo, hot, y_hi, y_lo):
    index_row = map_row(level, n_leaf, pos_ref, maps_ref, False)

    def emit(a, b, part):
        f_ref[pack_index(a, b)] = part

    extend_add(pk_ref, index_row, emit, last, u_hi, u_lo, hot, y_hi, y_lo)


def level_kernel(
    level, n_leaf, n_front, last, n_sib,
    pos_ref, base_ref, own_pk, maps_ref, *refs,
):
    mine_refs, theirs_refs, refs = refs[:PIECES], refs[PIECES : 2 * PIECES], refs[2 * PIECES :]
    sibs, (own_ref, next_ref, f_ref, x_ref, log_ref, tmp_ref, u_hi, u_lo, hot, y_hi, y_lo, *gathered) = (
        refs[:n_sib], refs[n_sib:],
    )
    core = pos_ref[1] & 1
    if n_sib == 1:
        sib_pk = sibs[0]
    else:
        sib_pk = gathered[0]
        sib_pk[pl.ds(core * (NPACK // 2), NPACK // 2)] = sibs[0][...]
        sib_pk[pl.ds((1 - core) * (NPACK // 2), NPACK // 2)] = sibs[1][...]
    index_row = map_row(level, n_leaf, pos_ref, maps_ref, True)
    where_is = {}
    bounds = piece_bounds(last)
    for owner in range(2):
        for n, block in enumerate(owned_blocks(owner, last)):
            p = max(m for m in range(PIECES) if bounds[m] <= n)
            where_is[block] = owner, p, n - bounds[p]

    def emit(a, b, part):
        per = TILE // T
        for r in range(per):
            for h in range(per):
                i, j = a * per + r, b * per + h
                if j > i:
                    continue
                owner, p, n = where_is[i, j]
                here, there = slice(i * T, (i + 1) * T), slice(j * T, (j + 1) * T)
                dense = jnp.where(core == owner, mine_refs[p][n], theirs_refs[p][n])
                mine, its = slice(r * T, (r + 1) * T), slice(h * T, (h + 1) * T)
                f_ref[here, there] = (base_ref[pack_index(a, b), mine, its] + part[mine, its]) + dense

    extend_add(sib_pk, index_row, emit, last, u_hi, u_lo, hot, y_hi, y_lo)
    factor_panel(f_ref, x_ref, log_ref, tmp_ref, WIDTH, NB)
    zero_above(f_ref, NB)
    rank = (pos_ref[0] & ((1 << level) - 1)) * n_front + pos_ref[1]
    write_own(own_ref, f_ref, rank * own_ref.shape[0])
    kids_log = own_pk[0][0:1, T - 1 : T] + sib_pk[0][0:1, T - 1 : T]
    log_value = kids_log + log_total(log_ref)
    if last:
        next_ref[...] = jnp.broadcast_to(log_value, next_ref.shape)
    else:

        def tail_of(i, j):
            return f_ref[SEP + i * T : SEP + (i + 1) * T, SEP + j * T : SEP + (j + 1) * T]

        write_update(next_ref, f_ref[SEP:, 0:SEP], tail_of, log_value)


def gather_rows(lists_ref, totals, local, core):
    block_ids = iota2((8, KC), 0).astype(F32)
    column_ids = [(iota2((16, KC), 0) + 16 * j).astype(F32).astype(BF16) for j in range(T // 16)]
    one, zero = jnp.ones((16, KC), BF16), jnp.zeros((16, KC), BF16)
    blank = jnp.zeros((8, KC), F32)
    pair_of = iota2((T, T), 1) % 64 // 16
    size = lists_ref.shape[1] - 8
    turn = local // T
    start = (2 * turn + ((turn + core) & 1)) * T + local % T
    for g in range(STEP // 8):
        hots, parts = [], ([], [])
        rank = (start + g * 8) // size
        at = pl.multiple_of((start + g * 8) % size, 8)
        cols = lists_ref[rank, pl.ds(at, 8), 0:KC]
        vals = lists_ref[rank, pl.ds(at, 8), KC:]
        block_no = jnp.floor(cols * (1.0 / T))
        within = cols - block_no * T
        for r in range(8):
            column = row_of(within, r)
            column = jnp.concatenate([column, column], axis=0).astype(BF16)
            hots.append(jnp.concatenate([jnp.where(ids == column, one, zero) for ids in column_ids], axis=0))
            val = row_of(vals, r)
            hi = val.astype(BF16).astype(F32)
            pick = block_ids == row_of(block_no, r)
            parts[0].append(jnp.where(pick, hi, 0.0))
            parts[1].append(jnp.where(pick, val - hi, 0.0))
        held = [
            jnp.concatenate(
                [
                    jnp.concatenate([part[r], blank] if side == 0 else [blank, part[r + 1]], axis=0).astype(BF16)
                    for part in parts
                    for r in range(0, 8, 2)
                ],
                axis=0,
            )
            for side in range(2)
        ]
        held = jnp.concatenate(held, axis=1)
        total = jnp.zeros((T, T), F32)
        for pair in range(4):
            streamed = jnp.concatenate([hots[2 * pair], hots[2 * pair + 1]], axis=1)
            total = jnp.where(pair_of == pair, dot_nt(streamed, held), total)
        totals[g] = total


def spread_rows(totals, dense, local):
    base = local // T * WIDTH + local % T
    for g in range(STEP // 8):
        flipped = totals[g].T
        both = flipped[0:64] + flipped[64:128]
        for r in range(8):
            dense[pl.ds(base + g * 8 + r, 8, stride=T), :] = both[8 * r : 8 * r + 8]


def pack_kernel(n_front, sizes, pos_ref, cols_ref, vals_ref, diag_ref, *refs):
    out_refs, line_ref = refs[:-1], refs[-1]
    line_ref[...] = jnp.zeros_like(line_ref)
    line_ref[0:1, 0 : diag_ref.shape[1]] = diag_ref[...]
    lane = iota2((8, 2 * KC), 1)
    offset = 0
    for n, (size, out_ref) in enumerate(zip(sizes, out_refs)):
        out_ref[0:size, 0:KC] = cols_ref[offset : offset + size, :].astype(F32)
        out_ref[0:size, KC:] = vals_ref[offset : offset + size, :]
        rank = (pos_ref[0] & ((2 << n) - 1)) * n_front + pos_ref[1]
        first = rank * size % T
        line = pltpu.roll(line_ref[...], (first - offset) & (2 * KC - 1), 1)
        line = jnp.broadcast_to(jnp.where((lane >= first) & (lane < first + size), line, 0.0)[0:1], (8, 2 * KC))
        out_ref[size : size + 8, :] = line
        offset += size


def params():
    return pltpu.CompilerParams(vmem_limit_bytes=VMEM_LIMIT)


def vmem():
    return pl.BlockSpec(memory_space=pltpu.VMEM)


def smem():
    return pl.BlockSpec(memory_space=pltpu.SMEM)


def shape(*dims):
    return jax.ShapeDtypeStruct(dims, F32)


def cost(us):
    return pl.CostEstimate(flops=0, bytes_accessed=int(us * 3.0e6), transcendentals=0)


def call(kernel, out_shape, n_args, n_smem, scratch, us, name):
    outs = out_shape if isinstance(out_shape, tuple) else (out_shape,)
    return pl.pallas_call(
        kernel,
        out_shape=out_shape,
        in_specs=[smem()] * n_smem + [vmem()] * (n_args - n_smem),
        out_specs=(vmem(),) * len(outs) if isinstance(out_shape, tuple) else vmem(),
        scratch_shapes=scratch,
        compiler_params=params(),
        cost_estimate=cost(us),
        name=name,
    )


def row_scratch():
    return pltpu.VMEM((9 * T, T), F32)


def extend_scratch():
    return [pltpu.VMEM((BND, BND), BF16)] * 2 + [pltpu.VMEM((WIDTH, BND), BF16)] * 3


def swap_front(x, mask):
    count = lax.axis_size("front")
    return lax.ppermute(x, "front", [(f, f ^ mask) for f in range(count)])


def hypercube(strip, masks):
    pieces = {0: strip}
    for mask in masks:
        for m in sorted(pieces):
            pieces[m | mask] = swap_front(pieces[m], mask)
    return [pieces[m] for m in range(len(pieces))]


def after(x, done):
    return lax.optimization_barrier((x, done))[0]


def body(leaf_bits, leaf_fronts, coupling_cols, coupling_vals, sep_diag, child_maps):
    n_front = lax.axis_size("front")
    bits = len(leaf_bits)
    n_leaf = 1 << bits
    front = lax.axis_index("front")
    leaf = lax.axis_index(leaf_bits)
    pos = jnp.stack([leaf, front]).astype(jnp.int32)
    strip = leaf_fronts[0]
    half = n_front // 2
    inner = [1 << b for b in range(half.bit_length() - 1)]
    strip_rows = WIDTH // n_front
    panel_strip = strip[:, :SEP]
    cross = swap_front(panel_strip, half)
    sizes = [WIDTH // (n_front << level) for level in range(1, bits + 1)]
    packed = call(
        functools.partial(pack_kernel, n_front, sizes),
        tuple(shape(size + 8, 2 * KC) for size in sizes), 4, 1, [pltpu.VMEM((8, 2 * KC), F32)], 1, "pack_lists",
    )(pos, coupling_cols[0, 0], coupling_vals[0, 0], sep_diag[0])
    panels = hypercube(panel_strip, inner) + hypercube(cross, inner)
    strip3 = after(strip, panels[-1])[:, SEP:]
    cross3 = lax.ppermute(strip3, "front", [(f, f - half) for f in range(half, n_front)])

    lists = []
    for n, size in enumerate(sizes):
        gathered = lax.all_gather(after(packed[n], cross), leaf_bits[bits - 1 - n :] + ("front",), axis=0, tiled=False)
        if size < 8:
            rows = gathered[:, :size].reshape(WIDTH // 8, 8, 2 * KC)
            diag = gathered[:, size].reshape(WIDTH // 8, 8 // size, 2 * KC).sum(1, keepdims=True)
            gathered = jnp.concatenate([rows, jnp.pad(diag, ((0, 0), (0, 7), (0, 0)))], axis=1)
        lists.append(gathered)

    fac, inv, logs = call(
        functools.partial(head_kernel, n_front),
        (shape(SEP, SEP), shape(SEP, T), shape(8, T)), 1 + n_front, 1, [row_scratch()], 300, "head_factor",
    )(pos, *panels)
    pieces3 = hypercube(strip3, inner) + hypercube(after(cross3, inv), inner)
    piece, below = call(
        functools.partial(below_kernel, n_front),
        (shape(strip_rows, SEP), shape(BND, SEP)), 3 + n_front, 1, [pltpu.VMEM((WIDTH, SEP), F32)],
        4, "leaf_below",
    )(pos, fac, inv, *panels)
    pk = call(
        functools.partial(update_kernel, n_front), shape(NPACK, T, T), 3 + n_front, 1,
        [pltpu.VMEM((BND, BND), F32)], 3, "leaf_update",
    )(pos, below, logs, *pieces3)
    pieces = [piece]
    for level in range(1, bits + 1):
        size = sizes[level - 1]
        last = level == bits
        axis = leaf_bits[bits - level]
        if level < 3:
            sibs = [lax.ppermute(pk, axis, [(0, 1), (1, 0)])]
        else:
            part = lax.dynamic_slice_in_dim(pk, (front & 1) * (NPACK // 2), NPACK // 2, 0)
            sibs = [lax.ppermute(part, axis, [(0, 1), (1, 0)])]
        bounds = piece_bounds(last)
        mine = call(
            functools.partial(coupling_kernel, last),
            tuple(shape(end - first, T, T) for first, end in zip(bounds, bounds[1:])), 2, 1,
            [pltpu.VMEM((NB * WIDTH, T), F32), pltpu.VMEM((STEP // 8, T, T), F32)], 0.2, "coupling",
        )(pos, after(lists[level - 1], pk))
        theirs = [swap_front(block, 1) for block in mine]
        base = call(
            functools.partial(own_kernel, level, n_leaf, last), shape(pack_index(WIDTH // TILE, 0), TILE, TILE), 3, 1, extend_scratch(), 0.2, "own_child",
        )(pos, pk, child_maps)
        if level >= 3:
            sibs.append(swap_front(after(sibs[0], base), 1))
        gathered = [pltpu.VMEM((NPACK, T, T), F32)] if len(sibs) == 2 else []
        piece, pk = call(
            functools.partial(level_kernel, level, n_leaf, n_front, last, len(sibs)),
            (shape(size, SEP), shape(8, T) if last else shape(NPACK, T, T)), 4 + 2 * PIECES + len(sibs), 1,
            [pltpu.VMEM((WIDTH, WIDTH), F32), pltpu.VMEM((SEP, T), F32), pltpu.VMEM((8, T), F32), row_scratch()]
            + extend_scratch() + gathered,
            300, "level_front",
        )(pos, base, pk, child_maps, *mine, *theirs, *sibs)
        pieces.append(piece)
    return jnp.concatenate(pieces, axis=0)[None, None], pk[0, 0]


def solution(mesh):
    bits = mesh.shape["leaf"].bit_length() - 1
    leaf_bits = tuple(f"leaf{b}" for b in reversed(range(bits)))
    fine = Mesh(mesh.devices.reshape((2,) * bits + (mesh.shape["front"],)), leaf_bits + ("front",))
    placed = (
        P(leaf_bits, "front", None),
        P(leaf_bits, "front", None, None),
        P(leaf_bits, "front", None, None),
        P(leaf_bits, "front", None),
        P(),
    )
    return jax.shard_map(
        functools.partial(body, leaf_bits),
        mesh=fine,
        in_specs=placed,
        out_specs=(P(leaf_bits, "front", None, None), P()),
        check_vma=False,
    )
```

profile of v0, /device:TPU:0, one launch (start us, length us, event | category | flops | bytes accessed | tf_op | source)
XLA Modules:
  0.0 190.6 jit_solution(18442614259040846779)
XLA Ops:
  7.2 1.1 slice.12.refs_0_
  8.3 3.0 %collective-permute-start.1 = (f32[256,512]{1,0:T(8,128)S(1)}, f32[256,512]{1,0:T(8,128)S(1)}, u32[]{:S(2)}, u32[]{:S(2)}) collective-permute-start(f32[256,512]{1,0:T(8,128)S(1)} %slice.12.refs_0_), channel_id=1, source_target_pairs={{0,2},{1,3},{2,0},{3,1},{4,6},{5,7},{6,4},{7,5},{8,10},{9,11},{10,... | collective-permute-start | bytes 1572872 | tf_op jit(solution)/shard_map/ppermute | solution.py:543
  11.4 0.9 copy-done.12
  12.3 0.9 copy-done.13
  13.8 1.3 pack_lists.1
  15.2 8.0 %collective-permute-done.1.refs_2_ = f32[256,512]{1,0:T(8,128)S(1)} collective-permute-done((f32[256,512]{1,0:T(8,128)S(1)}, f32[256,512]{1,0:T(8,128)S(1)}, u32[]{:S(2)}, u32[]{:S(2)}) %collective-permute-start.1) | collective-permute-done | bytes 524320 | tf_op jit(solution)/shard_map/ppermute | solution.py:543
  24.6 1.4 collective-permute-done.2.refs_3_
  26.0 1.1 slice.10.refs_0_
  27.1 1.3 collective-permute-start.4
  28.6 17.1 %head_factor.1 = (f32[512,512]{1,0:T(8,128)S(1)}, f32[512,128]{1,0:T(8,128)S(1)}, f32[8,128]{1,0:T(8,128)S(1)}) custom-call(s32[2]{0:T(128)S(1)} %pad_add_fusion.pos_ref, f32[256,512]{1,0:T(8,128)S(1)} %slice.12.refs_0_, f32[256,512]{1,0:T(8,128)S(1)} %collective-permute-done.refs_1_, f32[256,512]{1,0:T(8,128)S(1)} %collective-permute-done.1.refs_2_, ...), custom_call_target="tpu_custom_call" | custom-call | bytes 900000000 | tf_op jit(solution)/shard_map/head_factor/pallas_call | solution.py:589
  46.2 3.1 %leaf_below.1 = (f32[256,512]{1,0:T(8,128)S(1)}, f32[512,512]{1,0:T(8,128)S(1)}) custom-call(s32[2]{0:T(128)S(1)} %pad_add_fusion.pos_ref, f32[512,512]{1,0:T(8,128)S(1)} %get-tuple-element.34.fac, f32[512,128]{1,0:T(8,128)S(1)} %get-tuple-element.35.inv, f32[256,512]{1,0:T(8,128)S(1)} %slice.12.refs_0_, f32[256,512]{1,0:T(8,128)S(1)} %collective-permute-done.refs_1_, ...), custom_call_target="tpu_custom_call" | custom-call | bytes 12000000 | tf_op jit(solution)/shard_map/leaf_below/pallas_call | solution.py:594
  49.3 2.0 %leaf_update.1.pk_ref.own_pk = f32[10,128,128]{2,1,0:T(8,128)S(1)} custom-call(s32[2]{0:T(128)S(1)} %pad_add_fusion.pos_ref, f32[512,512]{1,0:T(8,128)S(1)} %get-tuple-element.37.below_ref, f32[8,128]{1,0:T(8,128)S(1)} %get-tuple-element.38.log_ref, f32[256,512]{1,0:T(8,128)S(1)} %slice.10.refs_0_, f32[256,512]{1,0:T(8,128)S(1)} %collective-permute-done.3.refs_1_, ...), custom_call_target="tpu_custom_call" | custom-call | bytes 9000000 | tf_op jit(solution)/shard_map/leaf_update/pallas_call | solution.py:599
  51.3 1.8 collective-permute-start.9
  53.1 1.2 copy-done.3
  54.4 9.6 %coupling.3 = (f32[6,128,128]{2,1,0:T(8,128)S(1)}, f32[6,128,128]{2,1,0:T(8,128)S(1)}, f32[6,128,128]{2,1,0:T(8,128)S(1)}) custom-call(s32[2]{0:T(128)S(1)} %pad_add_fusion.pos_ref, f32[8,136,256]{2,1,0:T(8,128)S(1)} %bitcast.14), custom_call_target="tpu_custom_call" | custom-call | bytes 600000 | tf_op jit(solution)/shard_map/coupling/pallas_call | solution.py:614
  64.7 4.1 %own_child.3.base_ref = f32[10,256,256]{2,1,0:T(8,128)S(1)} custom-call(s32[2]{0:T(128)S(1)} %pad_add_fusion.pos_ref, f32[10,128,128]{2,1,0:T(8,128)S(1)} %leaf_update.1.pk_ref.own_pk, s32[14,512]{1,0:T(8,128)S(1)} %copy-done.1), custom_call_target="tpu_custom_call" | custom-call | bytes 600000 | tf_op jit(solution)/shard_map/own_child/pallas_call | solution.py:620
  68.9 23.7 %level_front.3 = (f32[128,512]{1,0:T(8,128)S(1)}, f32[10,128,128]{2,1,0:T(8,128)S(1)}) custom-call(s32[2]{0:T(128)S(1)} %pad_add_fusion.pos_ref, f32[10,256,256]{2,1,0:T(8,128)S(1)} %own_child.3.base_ref, f32[10,128,128]{2,1,0:T(8,128)S(1)} %leaf_update.1.pk_ref.own_pk, s32[14,512]{1,0:T(8,128)S(1)} %copy-done.1, ...), custom_call_target="tpu_custom_call" | custom-call | bytes 900000000 | tf_op jit(solution)/shard_map/level_front/pallas_call | solution.py:626
  93.3 1.6 collective-permute-start.13
  94.9 1.3 copy-done.2
  96.1 9.5 %coupling.4 = (f32[6,128,128]{2,1,0:T(8,128)S(1)}, f32[6,128,128]{2,1,0:T(8,128)S(1)}, f32[6,128,128]{2,1,0:T(8,128)S(1)}) custom-call(s32[2]{0:T(128)S(1)} %pad_add_fusion.pos_ref, f32[16,72,256]{2,1,0:T(8,128)S(1)} %bitcast.13), custom_call_target="tpu_custom_call" | custom-call | bytes 600000 | tf_op jit(solution)/shard_map/coupling/pallas_call | solution.py:614
  106.3 4.3 %own_child.4.base_ref = f32[10,256,256]{2,1,0:T(8,128)S(1)} custom-call(s32[2]{0:T(128)S(1)} %pad_add_fusion.pos_ref, f32[10,128,128]{2,1,0:T(8,128)S(1)} %get-tuple-element.48.pk_ref.own_pk, s32[14,512]{1,0:T(8,128)S(1)} %copy-done.1), custom_call_target="tpu_custom_call" | custom-call | bytes 600000 | tf_op jit(solution)/shard_map/own_child/pallas_call | solution.py:620
  112.2 1.0 copy-done.7
  113.2 1.0 copy-done.9
  114.2 24.2 %level_front.4 = (f32[64,512]{1,0:T(8,128)S(1)}, f32[10,128,128]{2,1,0:T(8,128)S(1)}) custom-call(s32[2]{0:T(128)S(1)} %pad_add_fusion.pos_ref, f32[10,256,256]{2,1,0:T(8,128)S(1)} %own_child.4.base_ref, f32[10,128,128]{2,1,0:T(8,128)S(1)} %get-tuple-element.48.pk_ref.own_pk, s32[14,512]{1,0:T(8,128)S(1)} %copy-done.1, ...), custom_call_target="tpu_custom_call" | custom-call | bytes 900000000 | tf_op jit(solution)/shard_map/level_front/pallas_call | solution.py:626
  139.1 2.6 %collective-permute-start.17 = (f32[5,128,128]{2,1,0:T(8,128)}, f32[5,128,128]{2,1,0:T(8,128)}, u32[]{:S(2)}, u32[]{:S(2)}) collective-permute-start(f32[5,128,128]{2,1,0:T(8,128)} %constant_dynamic-slice_fusion), channel_id=1, source_target_pairs={{0,16},{16,0},{1,17},{17,1},{2,18},{18,2},{3,19},{19,3},{4,20},{20... | collective-permute-start | bytes 983048 | tf_op jit(solution)/shard_map/ppermute | solution.py:612
  141.7 3.7 %own_child.5.base_ref = f32[10,256,256]{2,1,0:T(8,128)S(1)} custom-call(s32[2]{0:T(128)S(1)} %pad_add_fusion.pos_ref, f32[10,128,128]{2,1,0:T(8,128)S(1)} %get-tuple-element.56.pk_ref.own_pk, s32[14,512]{1,0:T(8,128)S(1)} %copy-done.1), custom_call_target="tpu_custom_call" | custom-call | bytes 600000 | tf_op jit(solution)/shard_map/own_child/pallas_call | solution.py:620
  145.5 1.3 copy-done
  146.8 9.1 %coupling.5 = (f32[4,128,128]{2,1,0:T(8,128)S(1)}, f32[4,128,128]{2,1,0:T(8,128)S(1)}, f32[5,128,128]{2,1,0:T(8,128)S(1)}) custom-call(s32[2]{0:T(128)S(1)} %pad_add_fusion.pos_ref, f32[32,40,256]{2,1,0:T(8,128)S(1)} %bitcast.12), custom_call_target="tpu_custom_call" | custom-call | bytes 600000 | tf_op jit(solution)/shard_map/coupling/pallas_call | solution.py:614
  156.0 1.3 collective-permute-done.17.refs_6_
  157.8 1.4 collective-permute-done.14.refs_3_
  159.6 22.9 %level_front.5 = (f32[32,512]{1,0:T(8,128)S(1)}, f32[8,128]{1,0:T(8,128)S(1)}) custom-call(s32[2]{0:T(128)S(1)} %pad_add_fusion.pos_ref, f32[10,256,256]{2,1,0:T(8,128)S(1)} %own_child.5.base_ref, f32[10,128,128]{2,1,0:T(8,128)S(1)} %get-tuple-element.56.pk_ref.own_pk, s32[14,512]{1,0:T(8,128)S(1)} %copy-done.1, ...), custom_call_target="tpu_custom_call" | custom-call | bytes 900000000 | tf_op jit(solution)/shard_map/level_front/pallas_call | solution.py:626
  183.0 1.0 maximum_bitcast_fusion
  (64 shorter events, 8.8 us)
Async XLA Ops:
  7.2 46.0 %all-gather.7.cloned.1.call-start = ((), (), s32[]{:S(2)}) async-start(), calls=%async_computation | async-start | bytes 1253376 | tf_op jit(solution)/shard_map/all_gather | solution.py:582
  8.3 14.9 %collective-permute-start.1 = (f32[256,512]{1,0:T(8,128)S(1)}, f32[256,512]{1,0:T(8,128)S(1)}, u32[]{:S(2)}, u32[]{:S(2)}) collective-permute-start(f32[256,512]{1,0:T(8,128)S(1)} %slice.12.refs_0_), channel_id=1, source_target_pairs={{0,2},{1,3},{2,0},{3,1},{4,6},{5,7},{6,4},{7,5},{8,10},{9,11},{10,... | collective-permute-start | bytes 1572872 | tf_op jit(solution)/shard_map/ppermute | solution.py:543
  11.4 0.9 copy-start.12
  23.2 71.6 %all-gather.9.cloned.1.call-start = ((), (), s32[]{:S(2)}) async-start(), calls=%async_computation.1 | async-start | bytes 1253376 | tf_op jit(solution)/shard_map/all_gather | solution.py:582
  24.0 121.4 %all-gather.11.cloned.1.call-start = ((), (), s32[]{:S(2)}) async-start(), calls=%async_computation.2 | async-start | bytes 1351680 | tf_op jit(solution)/shard_map/all_gather | solution.py:582
  24.0 2.0 %collective-permute-start.2 = (f32[256,512]{1,0:T(8,128)S(1)}, f32[256,512]{1,0:T(8,128)S(1)}, u32[]{:S(2)}, u32[]{:S(2)}) collective-permute-start(f32[256,512]{1,0:T(8,128)S(1)} %collective-permute-done.1.refs_2_), channel_id=1, source_target_pairs={{0,1},{1,0},{2,3},{3,2},{4,5},{5,4},{6,7},{7,6},{8,9},{9,8},{10,11... | collective-permute-start | bytes 1572872 | tf_op jit(solution)/shard_map/ppermute | solution.py:543
  24.1 4.5 %collective-permute-start = (f32[256,512]{1,0:T(8,128)S(1)}, f32[256,512]{1,0:T(8,128)S(1)}, u32[]{:S(2)}, u32[]{:S(2)}) collective-permute-start(f32[256,512]{1,0:T(8,128)S(1)} %slice.12.refs_0_), channel_id=1, source_target_pairs={{0,1},{1,0},{2,3},{3,2},{4,5},{5,4},{6,7},{7,6},{8,9},{9,8},{10,11... | collective-permute-start | bytes 1572872 | tf_op jit(solution)/shard_map/ppermute | solution.py:543
  27.1 18.6 %collective-permute-start.4 = (f32[256,512]{1,0:T(8,128)S(1)}, f32[256,512]{1,0:T(8,128)S(1)}, u32[]{:S(2)}, u32[]{:S(2)}) collective-permute-start(f32[256,512]{1,0:T(8,128)S(1)} %slice.10.refs_0_), channel_id=1, source_target_pairs={{2,0},{3,1},{6,4},{7,5},{10,8},{11,9},{14,12},{15,13},{18,16},{19,... | collective-permute-start | bytes 1572872 | tf_op jit(solution)/shard_map/ppermute | solution.py:578
  28.4 20.9 %collective-permute-start.3 = (f32[256,512]{1,0:T(8,128)S(1)}, f32[256,512]{1,0:T(8,128)S(1)}, u32[]{:S(2)}, u32[]{:S(2)}) collective-permute-start(f32[256,512]{1,0:T(8,128)S(1)} %slice.10.refs_0_), channel_id=1, source_target_pairs={{0,1},{1,0},{2,3},{3,2},{4,5},{5,4},{6,7},{7,6},{8,9},{9,8},{10,11... | collective-permute-start | bytes 1572872 | tf_op jit(solution)/shard_map/ppermute | solution.py:543
  45.7 3.6 %collective-permute-start.5 = (f32[256,512]{1,0:T(8,128)S(1)}, f32[256,512]{1,0:T(8,128)S(1)}, u32[]{:S(2)}, u32[]{:S(2)}) collective-permute-start(f32[256,512]{1,0:T(8,128)S(1)} %collective-permute-done.4.refs_2_), channel_id=1, source_target_pairs={{0,1},{1,0},{2,3},{3,2},{4,5},{5,4},{6,7},{7,6},{8,9},{9,8},{10,11... | collective-permute-start | bytes 1572872 | tf_op jit(solution)/shard_map/ppermute | solution.py:543
  49.3 2.0 %copy-start.4 = (f32[256,512]{1,0:T(8,128)}, f32[256,512]{1,0:T(8,128)S(1)}, u32[]{:S(2)}) copy-start(f32[256,512]{1,0:T(8,128)S(1)} %get-tuple-element.36) | copy-start | bytes 1572868
  49.3 15.4 %copy-start.1 = (s32[14,512]{1,0:T(8,128)S(1)}, s32[14,512]{1,0:T(8,128)}, u32[]{:S(2)}) copy-start(s32[14,512]{1,0:T(8,128)} %maps_ref.11) | copy-start | bytes 86020
  51.3 17.5 %collective-permute-start.9 = (f32[10,128,128]{2,1,0:T(8,128)S(1)}, f32[10,128,128]{2,1,0:T(8,128)S(1)}, u32[]{:S(2)}, u32[]{:S(2)}) collective-permute-start(f32[10,128,128]{2,1,0:T(8,128)S(1)} %leaf_update.1.pk_ref.own_pk), channel_id=1, source_target_pairs={{0,4},{4,0},{1,5},{5,1},{2,6},{6,2},{3,7},{7,3},{8,12},{12,8},{9,1... | collective-permute-start | bytes 1966088 | tf_op jit(solution)/shard_map/ppermute | solution.py:609
  53.1 1.2 copy-start.3
  64.0 4.8 %collective-permute-start.6 = (f32[6,128,128]{2,1,0:T(8,128)S(1)}, f32[6,128,128]{2,1,0:T(8,128)S(1)}, u32[]{:S(2)}, u32[]{:S(2)}) collective-permute-start(f32[6,128,128]{2,1,0:T(8,128)S(1)} %get-tuple-element.44.refs_0_), channel_id=1, source_target_pairs={{0,1},{1,0},{2,3},{3,2},{4,5},{5,4},{6,7},{7,6},{8,9},{9,8},{10,11... | collective-permute-start | bytes 1179656 | tf_op jit(solution)/shard_map/ppermute | solution.py:543
  64.1 4.7 %collective-permute-start.7 = (f32[6,128,128]{2,1,0:T(8,128)S(1)}, f32[6,128,128]{2,1,0:T(8,128)S(1)}, u32[]{:S(2)}, u32[]{:S(2)}) collective-permute-start(f32[6,128,128]{2,1,0:T(8,128)S(1)} %get-tuple-element.45.refs_1_), channel_id=1, source_target_pairs={{0,1},{1,0},{2,3},{3,2},{4,5},{5,4},{6,7},{7,6},{8,9},{9,8},{10,11... | collective-permute-start | bytes 1179656 | tf_op jit(solution)/shard_map/ppermute | solution.py:543
  64.6 4.2 %collective-permute-start.8 = (f32[6,128,128]{2,1,0:T(8,128)S(1)}, f32[6,128,128]{2,1,0:T(8,128)S(1)}, u32[]{:S(2)}, u32[]{:S(2)}) collective-permute-start(f32[6,128,128]{2,1,0:T(8,128)S(1)} %get-tuple-element.46.refs_2_), channel_id=1, source_target_pairs={{0,1},{1,0},{2,3},{3,2},{4,5},{5,4},{6,7},{7,6},{8,9},{9,8},{10,11... | collective-permute-start | bytes 1179656 | tf_op jit(solution)/shard_map/ppermute | solution.py:543
  93.3 18.9 %collective-permute-start.13 = (f32[10,128,128]{2,1,0:T(8,128)S(1)}, f32[10,128,128]{2,1,0:T(8,128)S(1)}, u32[]{:S(2)}, u32[]{:S(2)}) collective-permute-start(f32[10,128,128]{2,1,0:T(8,128)S(1)} %get-tuple-element.48.pk_ref.own_pk), channel_id=1, source_target_pairs={{0,8},{8,0},{1,9},{9,1},{2,10},{10,2},{3,11},{11,3},{4,12},{12,4},... | collective-permute-start | bytes 1966088 | tf_op jit(solution)/shard_map/ppermute | solution.py:609
  94.9 1.3 copy-start.2
  105.6 5.1 %collective-permute-start.10 = (f32[6,128,128]{2,1,0:T(8,128)S(1)}, f32[6,128,128]{2,1,0:T(8,128)S(1)}, u32[]{:S(2)}, u32[]{:S(2)}) collective-permute-start(f32[6,128,128]{2,1,0:T(8,128)S(1)} %get-tuple-element.52.refs_0_), channel_id=1, source_target_pairs={{0,1},{1,0},{2,3},{3,2},{4,5},{5,4},{6,7},{7,6},{8,9},{9,8},{10,11... | collective-permute-start | bytes 1179656 | tf_op jit(solution)/shard_map/ppermute | solution.py:543
  105.8 5.6 %collective-permute-start.11 = (f32[6,128,128]{2,1,0:T(8,128)S(1)}, f32[6,128,128]{2,1,0:T(8,128)S(1)}, u32[]{:S(2)}, u32[]{:S(2)}) collective-permute-start(f32[6,128,128]{2,1,0:T(8,128)S(1)} %get-tuple-element.53.refs_1_), channel_id=1, source_target_pairs={{0,1},{1,0},{2,3},{3,2},{4,5},{5,4},{6,7},{7,6},{8,9},{9,8},{10,11... | collective-permute-start | bytes 1179656 | tf_op jit(solution)/shard_map/ppermute | solution.py:543
  106.2 6.0 %collective-permute-start.12 = (f32[6,128,128]{2,1,0:T(8,128)S(1)}, f32[6,128,128]{2,1,0:T(8,128)}, u32[]{:S(2)}, u32[]{:S(2)}) collective-permute-start(f32[6,128,128]{2,1,0:T(8,128)S(1)} %get-tuple-element.54.refs_2_), channel_id=1, source_target_pairs={{0,1},{1,0},{2,3},{3,2},{4,5},{5,4},{6,7},{7,6},{8,9},{9,8},{10,11... | collective-permute-start | bytes 1179656 | tf_op jit(solution)/shard_map/ppermute | solution.py:543
  112.2 1.0 copy-start.7
  113.2 1.0 copy-start.9
  139.1 18.1 %collective-permute-start.17 = (f32[5,128,128]{2,1,0:T(8,128)}, f32[5,128,128]{2,1,0:T(8,128)}, u32[]{:S(2)}, u32[]{:S(2)}) collective-permute-start(f32[5,128,128]{2,1,0:T(8,128)} %constant_dynamic-slice_fusion), channel_id=1, source_target_pairs={{0,16},{16,0},{1,17},{17,1},{2,18},{18,2},{3,19},{19,3},{4,20},{20... | collective-permute-start | bytes 983048 | tf_op jit(solution)/shard_map/ppermute | solution.py:612
  145.4 1.3 copy-start
  155.8 3.8 %collective-permute-start.16 = (f32[5,128,128]{2,1,0:T(8,128)S(1)}, f32[5,128,128]{2,1,0:T(8,128)S(1)}, u32[]{:S(2)}, u32[]{:S(2)}) collective-permute-start(f32[5,128,128]{2,1,0:T(8,128)S(1)} %get-tuple-element.62.refs_2_), channel_id=1, source_target_pairs={{0,1},{1,0},{2,3},{3,2},{4,5},{5,4},{6,7},{7,6},{8,9},{9,8},{10,11... | collective-permute-start | bytes 983048 | tf_op jit(solution)/shard_map/ppermute | solution.py:543
  157.2 2.4 %collective-permute-start.18 = (f32[5,128,128]{2,1,0:T(8,128)}, f32[5,128,128]{2,1,0:T(8,128)S(1)}, u32[]{:S(2)}, u32[]{:S(2)}) collective-permute-start(f32[5,128,128]{2,1,0:T(8,128)} %collective-permute-done.17.refs_6_), channel_id=1, source_target_pairs={{0,1},{1,0},{2,3},{3,2},{4,5},{5,4},{6,7},{7,6},{8,9},{9,8},{10,11... | collective-permute-start | bytes 983048 | tf_op jit(solution)/shard_map/ppermute | solution.py:543
  157.3 1.9 %collective-permute-start.14 = (f32[4,128,128]{2,1,0:T(8,128)S(1)}, f32[4,128,128]{2,1,0:T(8,128)S(1)}, u32[]{:S(2)}, u32[]{:S(2)}) collective-permute-start(f32[4,128,128]{2,1,0:T(8,128)S(1)} %get-tuple-element.60.refs_0_), channel_id=1, source_target_pairs={{0,1},{1,0},{2,3},{3,2},{4,5},{5,4},{6,7},{7,6},{8,9},{9,8},{10,11... | collective-permute-start | bytes 786440 | tf_op jit(solution)/shard_map/ppermute | solution.py:543
  157.7 25.3 %copy-start.5 = (f32[256,512]{1,0:T(8,128)S(1)}, f32[256,512]{1,0:T(8,128)}, u32[]{:S(2)}) copy-start(f32[256,512]{1,0:T(8,128)} %copy-done.4) | copy-start | bytes 1572868
  157.7 25.3 %copy-start.11 = (f32[128,512]{1,0:T(8,128)S(1)}, f32[128,512]{1,0:T(8,128)}, u32[]{:S(2)}) copy-start(f32[128,512]{1,0:T(8,128)} %copy-done.10) | copy-start | bytes 786436
  157.7 1.9 collective-permute-start.15
  (5 other events, 3.8 us)
Sparse Core Ops, SparseCore 0:
  23.4 26.8 all-gather.6
  51.9 31.3 all-gather.8
  86.1 54.2 all-gather.10
where the time goes:
time: 194 us; the launch traced here: 191 us
  Pallas kernels  135 us (70%)
  between operations  14 us (7%)
  local copies, waits for them, and re-layouts  13.9 us (7%)
  starting transfers between devices  13.7 us (7%)
  waiting for transfers between devices  13.3 us (7%)
    pallas_call x3, Pallas kernels, body(): call(functools.partial(level_kernel, level, n_leaf, n_front, last, len(si...  70.8 us
    pallas_call x3, Pallas kernels, body(): call(functools.partial(coupling_kernel, last), tuple((shape(end - first,...  28.2 us
    pallas_call x1, Pallas kernels, body(): call(functools.partial(head_kernel, n_front), (shape(SEP, SEP), shape(SEP...  17.1 us
    pallas_call x3, Pallas kernels, body(): call(functools.partial(own_kernel, level, n_leaf, last), shape(pack_index...  12.1 us
    ppermute x15, waiting for transfers between devices, swap_front(): return lax.ppermute(x, 'front', [(f, f ^ mask) for f in range(count)])  11.3 us
    unnamed x30, local copies, waits for them, and re-layouts  10.5 us
    ppermute x15, starting transfers between devices, swap_front(): return lax.ppermute(x, 'front', [(f, f ^ mask) for f in range(count)])  6.28 us
  transfers between devices with their start and end apart: 22, of which 5 were waited for; matrix products, arithmetic and copies ran while one was open for 1% of the time, Pallas kernels for 59%

commit v1 on v0

--- a/solution.py
+++ b/solution.py
@@ -15,12 +15,12 @@
 NB = SEP // T
 PANEL = 32
 PIECES = 3
-STEP = 32
+STEP = 64
 TILE = 256
 NPACK = NB * (NB + 1) // 2
 F32 = jnp.float32
 BF16 = jnp.bfloat16
-VMEM_LIMIT = 28 * 1024 * 1024
+VMEM_LIMIT = 16 * 1024 * 1024
 
 
 def pack_index(i, j):
@@ -92,6 +92,9 @@
     upper_acc = jnp.zeros((8, T), F32)
     inv_acc = jnp.zeros((8, T), F32)
     to_p, to_q, first = {}, {}, {}
+    if s + 1 < keep:
+        near = [lane_of(groups[s + 1], c + k) for k in range(8)]
+        following = jnp.where(inside, 0.0, groups[s + 1])
 
     def emit(k, line, entries, root):
         inv_row = line * root
@@ -121,9 +124,16 @@
         for i in rest:
             to_p[p, i], to_q[p, i] = w[i] * recip, z[i] * recip
             rows[i] = rows[i] - (to_p[p, i] * rows[p] + to_q[p, i] * rows[q])
+        if s + 1 < keep:
+            near_p, near_q = (e * near[p] - b * near[q]) * recip, (a * near[q] - b * near[p]) * recip
+            following = following - (near_p * rows[p] + near_q * rows[q])
+            for m in rest:
+                near[m] = near[m] - (near_p * d[p, m] + near_q * d[q, m])
         first[p] = (e * rows[p] - b * rows[q]) * recip
         first[q] = (a * rows[q] - b * rows[p]) * recip
     if s + 1 < keep:
+        groups[s + 1] = following
+    if s + 2 < keep:
         sol = [None] * 8
         for p in (6, 4, 2, 0):
             rest = range(p + 2, 8)
@@ -131,7 +141,7 @@
             if p < 6:
                 sol[p] = sol[p] - tree_sum([to_p[p, m] * sol[m] for m in rest])
                 sol[p + 1] = sol[p + 1] - tree_sum([to_q[p, m] * sol[m] for m in rest])
-        for g in range(s + 1, keep):
+        for g in range(s + 2, keep):
             old = groups[g]
             groups[g] = jnp.where(inside, 0.0, old) - tree_sum([lane_of(old, c + k) * sol[k] for k in range(8)])
     return jnp.where(lane >= c + sub, upper_acc, 0.0), jnp.where(lane <= c + sub, inv_acc, 0.0)
@@ -332,24 +342,36 @@
 
 
 def coupling_kernel(last, pos_ref, lists_ref, *refs):
-    out_refs, (dense, totals) = refs[:-2], refs[-2:]
+    out_refs, (dense, held_ref, sems) = refs[:-3], refs[-3:]
     bounds = piece_bounds(last)
     core = pos_ref[1] & 1
     size = lists_ref.shape[1] - 8
+    ranks = T // size
     eye = iota2((T, T), 0) == iota2((T, T), 1)
     limit = NB if last else 2 * NB
-    steps = WIDTH // 2 // STEP
-
-    @pl.loop(0, steps + 1)
+
+    def fetch(turn):
+        i = 2 * turn + ((turn + core) & 1)
+        return pltpu.make_async_copy(lists_ref.at[pl.ds(i * ranks, ranks)], held_ref.at[turn], sems.at[turn])
+
+    for turn in range(NB):
+        fetch(turn).start()
+
+    @pl.loop(0, NB * T // STEP)
     def _(step):
-        spread_rows(totals, dense, jnp.maximum(step - 1, 0) * STEP)
-        gather_rows(lists_ref, totals, jnp.minimum(step, steps - 1) * STEP, core)
+        turn = step // (T // STEP)
+
+        @pl.when(step % (T // STEP) == 0)
+        def _():
+            fetch(turn).wait()
+
+        spread_rows(held_ref, dense, turn, step % (T // STEP) * STEP)
 
     def turn_of(turn, offset):
         i = 2 * turn + ((turn + core) & 1)
         diag = jnp.zeros((1, T), F32)
-        for n in range(max(1, T // size)):
-            diag = diag + lists_ref[i * T // size + n, size : size + 1, 0:T]
+        for n in range(ranks):
+            diag = diag + held_ref[turn, n, size : size + 1, 0:T]
         for j in range(limit):
             for first, end, out_ref in zip(bounds, bounds[1:], out_refs):
 
@@ -360,7 +382,7 @@
 
         return offset + jnp.minimum(i + 1, limit)
 
-    lax.fori_loop(0, WIDTH // T // 2, turn_of, 0)
+    lax.fori_loop(0, NB, turn_of, 0)
 
 
 def own_kernel(level, n_leaf, last, pos_ref, pk_ref, maps_ref, f_ref, u_hi, u_lo, hot, y_hi, y_lo):
@@ -425,21 +447,19 @@
         write_update(next_ref, f_ref[SEP:, 0:SEP], tail_of, log_value)
 
 
-def gather_rows(lists_ref, totals, local, core):
+def spread_rows(lists_ref, dense, turn, first):
     block_ids = iota2((8, KC), 0).astype(F32)
     column_ids = [(iota2((16, KC), 0) + 16 * j).astype(F32).astype(BF16) for j in range(T // 16)]
     one, zero = jnp.ones((16, KC), BF16), jnp.zeros((16, KC), BF16)
     blank = jnp.zeros((8, KC), F32)
     pair_of = iota2((T, T), 1) % 64 // 16
-    size = lists_ref.shape[1] - 8
-    turn = local // T
-    start = (2 * turn + ((turn + core) & 1)) * T + local % T
+    size = lists_ref.shape[2] - 8
     for g in range(STEP // 8):
         hots, parts = [], ([], [])
-        rank = (start + g * 8) // size
-        at = pl.multiple_of((start + g * 8) % size, 8)
-        cols = lists_ref[rank, pl.ds(at, 8), 0:KC]
-        vals = lists_ref[rank, pl.ds(at, 8), KC:]
+        rank = (first + g * 8) // size
+        at = pl.multiple_of((first + g * 8) % size, 8)
+        cols = lists_ref[turn, rank, pl.ds(at, 8), 0:KC]
+        vals = lists_ref[turn, rank, pl.ds(at, 8), KC:]
         block_no = jnp.floor(cols * (1.0 / T))
         within = cols - block_no * T
         for r in range(8):
@@ -467,16 +487,10 @@
         for pair in range(4):
             streamed = jnp.concatenate([hots[2 * pair], hots[2 * pair + 1]], axis=1)
             total = jnp.where(pair_of == pair, dot_nt(streamed, held), total)
-        totals[g] = total
-
-
-def spread_rows(totals, dense, local):
-    base = local // T * WIDTH + local % T
-    for g in range(STEP // 8):
-        flipped = totals[g].T
+        flipped = total.T
         both = flipped[0:64] + flipped[64:128]
         for r in range(8):
-            dense[pl.ds(base + g * 8 + r, 8, stride=T), :] = both[8 * r : 8 * r + 8]
+            dense[pl.ds(turn * WIDTH + first + g * 8 + r, 8, stride=T), :] = both[8 * r : 8 * r + 8]
 
 
 def pack_kernel(n_front, sizes, pos_ref, cols_ref, vals_ref, diag_ref, *refs):
@@ -611,10 +625,20 @@
             part = lax.dynamic_slice_in_dim(pk, (front & 1) * (NPACK // 2), NPACK // 2, 0)
             sibs = [lax.ppermute(part, axis, [(0, 1), (1, 0)])]
         bounds = piece_bounds(last)
-        mine = call(
+        ranks = T // (lists[level - 1].shape[1] - 8)
+        mine = pl.pallas_call(
             functools.partial(coupling_kernel, last),
-            tuple(shape(end - first, T, T) for first, end in zip(bounds, bounds[1:])), 2, 1,
-            [pltpu.VMEM((NB * WIDTH, T), F32), pltpu.VMEM((STEP // 8, T, T), F32)], 0.2, "coupling",
+            out_shape=tuple(shape(end - first, T, T) for first, end in zip(bounds, bounds[1:])),
+            in_specs=[smem(), pl.BlockSpec(memory_space=pltpu.HBM)],
+            out_specs=(vmem(),) * PIECES,
+            scratch_shapes=[
+                pltpu.VMEM((NB * WIDTH, T), F32),
+                pltpu.VMEM((NB, ranks) + lists[level - 1].shape[1:], F32),
+                pltpu.SemaphoreType.DMA((NB,)),
+            ],
+            compiler_params=params(),
+            cost_estimate=cost(0.2),
+            name="coupling",
         )(pos, after(lists[level - 1], pk))
         theirs = [swap_front(block, 1) for block in mine]
         base = call(

time: 194 us -> 189 us (0.974); the launches traced: 191 us -> 189 us
  Pallas kernels: 135 us -> 126 us
  waiting for transfers between devices: 13.3 us -> 19.6 us
    all_gather x3, waiting for transfers between devices: 0.02 us -> 6.93 us  [body(): lax.all_gather(after(packed[n], cross), leaf_bits[bits - 1 - n:] + ('fron...]
    pallas_call x3, Pallas kernels: 70.8 us -> 66.2 us  [body(): call(functools.partial(level_kernel, level, n_leaf, n_front, last, len(si...]
    pallas_call x3, Pallas kernels: 28.2 us -> 26 us  [body(): pl.pallas_call(functools.partial(coupling_kernel, last), out_shape=tuple(...]
  transfers between devices with their start and end apart: 22 -> 22, of which waited for: 5 -> 7; matrix products, arithmetic and copies ran while one was open for 1% -> 1% of each run, Pallas kernels for 59% -> 56%
where the time goes in v1:
time: 189 us
  Pallas kernels  126 us (67%)
  waiting for transfers between devices  19.6 us (10%)
  between operations  14 us (7%)
  starting transfers between devices  13.9 us (7%)
  local copies, waits for them, and re-layouts  13.9 us (7%)
    pallas_call x3, Pallas kernels, body(): call(functools.partial(level_kernel, level, n_leaf, n_front, last, len(si...  66.2 us
    pallas_call x3, Pallas kernels, body(): pl.pallas_call(functools.partial(coupling_kernel, last), out_shape=tuple(...  26 us
    pallas_call x1, Pallas kernels, body(): call(functools.partial(head_kernel, n_front), (shape(SEP, SEP), shape(SEP...  15.6 us
    pallas_call x3, Pallas kernels, body(): call(functools.partial(own_kernel, level, n_leaf, last), shape(pack_index...  12.1 us
    ppermute x15, waiting for transfers between devices, swap_front(): return lax.ppermute(x, 'front', [(f, f ^ mask) for f in range(count)])  11.3 us
    unnamed x30, local copies, waits for them, and re-layouts  10.5 us
    all_gather x3, waiting for transfers between devices, body(): lax.all_gather(after(packed[n], cross), leaf_bits[bits - 1 - n:] + ('fron...  6.93 us
    ppermute x15, starting transfers between devices, swap_front(): return lax.ppermute(x, 'front', [(f, f ^ mask) for f in range(count)])  6.35 us
  transfers between devices with their start and end apart: 22, of which 7 were waited for; matrix products, arithmetic and copies ran while one was open for 1% of the time, Pallas kernels for 56%

profile of v1, /device:TPU:0, one launch (start us, length us, event | category | flops | bytes accessed | tf_op | source)
XLA Modules:
  0.0 188.7 jit_solution(9376542211279022323)
XLA Ops:
  7.2 1.1 slice.12.refs_0_
  8.3 3.0 %collective-permute-start.1 = (f32[256,512]{1,0:T(8,128)S(1)}, f32[256,512]{1,0:T(8,128)S(1)}, u32[]{:S(2)}, u32[]{:S(2)}) collective-permute-start(f32[256,512]{1,0:T(8,128)S(1)} %slice.12.refs_0_), channel_id=1, source_target_pairs={{0,2},{1,3},{2,0},{3,1},{4,6},{5,7},{6,4},{7,5},{8,10},{9,11},{10,... | collective-permute-start | bytes 1572872 | tf_op jit(solution)/shard_map/ppermute | solution.py:557
  11.4 0.9 copy-done.12
  12.3 0.9 copy-done.13
  13.8 1.3 pack_lists.1
  15.2 8.0 %collective-permute-done.1.refs_2_ = f32[256,512]{1,0:T(8,128)S(1)} collective-permute-done((f32[256,512]{1,0:T(8,128)S(1)}, f32[256,512]{1,0:T(8,128)S(1)}, u32[]{:S(2)}, u32[]{:S(2)}) %collective-permute-start.1) | collective-permute-done | bytes 524320 | tf_op jit(solution)/shard_map/ppermute | solution.py:557
  24.6 1.4 collective-permute-done.2.refs_3_
  26.0 1.1 slice.10.refs_0_
  27.1 1.3 collective-permute-start.4
  28.6 15.6 %head_factor.1 = (f32[512,512]{1,0:T(8,128)S(1)}, f32[512,128]{1,0:T(8,128)S(1)}, f32[8,128]{1,0:T(8,128)S(1)}) custom-call(s32[2]{0:T(128)S(1)} %pad_add_fusion.pos_ref, f32[256,512]{1,0:T(8,128)S(1)} %slice.12.refs_0_, f32[256,512]{1,0:T(8,128)S(1)} %collective-permute-done.refs_1_, f32[256,512]{1,0:T(8,128)S(1)} %collective-permute-done.1.refs_2_, ...), custom_call_target="tpu_custom_call" | custom-call | bytes 900000000 | tf_op jit(solution)/shard_map/head_factor/pallas_call | solution.py:603
  44.6 3.1 %leaf_below.1 = (f32[256,512]{1,0:T(8,128)S(1)}, f32[512,512]{1,0:T(8,128)S(1)}) custom-call(s32[2]{0:T(128)S(1)} %pad_add_fusion.pos_ref, f32[512,512]{1,0:T(8,128)S(1)} %get-tuple-element.34.fac, f32[512,128]{1,0:T(8,128)S(1)} %get-tuple-element.35.inv, f32[256,512]{1,0:T(8,128)S(1)} %slice.12.refs_0_, f32[256,512]{1,0:T(8,128)S(1)} %collective-permute-done.refs_1_, ...), custom_call_target="tpu_custom_call" | custom-call | bytes 12000000 | tf_op jit(solution)/shard_map/leaf_below/pallas_call | solution.py:608
  47.8 2.0 %leaf_update.1.pk_ref.own_pk = f32[10,128,128]{2,1,0:T(8,128)S(1)} custom-call(s32[2]{0:T(128)S(1)} %pad_add_fusion.pos_ref, f32[512,512]{1,0:T(8,128)S(1)} %get-tuple-element.37.below_ref, f32[8,128]{1,0:T(8,128)S(1)} %get-tuple-element.38.log_ref, f32[256,512]{1,0:T(8,128)S(1)} %slice.10.refs_0_, f32[256,512]{1,0:T(8,128)S(1)} %collective-permute-done.3.refs_1_, ...), custom_call_target="tpu_custom_call" | custom-call | bytes 9000000 | tf_op jit(solution)/shard_map/leaf_update/pallas_call | solution.py:613
  49.8 1.8 collective-permute-start.9
  51.6 1.2 copy-done.3
  52.8 8.8 %coupling.3 = (f32[6,128,128]{2,1,0:T(8,128)S(1)}, f32[6,128,128]{2,1,0:T(8,128)S(1)}, f32[6,128,128]{2,1,0:T(8,128)S(1)}) custom-call(s32[2]{0:T(128)S(1)} %pad_add_fusion.pos_ref, f32[8,136,256]{2,1,0:T(8,128)S(1)} %bitcast.14), custom_call_target="tpu_custom_call" | custom-call | bytes 600000 | tf_op jit(solution)/shard_map/coupling/pallas_call | solution.py:629
  62.4 4.1 %own_child.3.base_ref = f32[10,256,256]{2,1,0:T(8,128)S(1)} custom-call(s32[2]{0:T(128)S(1)} %pad_add_fusion.pos_ref, f32[10,128,128]{2,1,0:T(8,128)S(1)} %leaf_update.1.pk_ref.own_pk, s32[14,512]{1,0:T(8,128)S(1)} %copy-done.1), custom_call_target="tpu_custom_call" | custom-call | bytes 600000 | tf_op jit(solution)/shard_map/own_child/pallas_call | solution.py:644
  66.8 22.2 %level_front.3 = (f32[128,512]{1,0:T(8,128)S(1)}, f32[10,128,128]{2,1,0:T(8,128)S(1)}) custom-call(s32[2]{0:T(128)S(1)} %pad_add_fusion.pos_ref, f32[10,256,256]{2,1,0:T(8,128)S(1)} %own_child.3.base_ref, f32[10,128,128]{2,1,0:T(8,128)S(1)} %leaf_update.1.pk_ref.own_pk, s32[14,512]{1,0:T(8,128)S(1)} %copy-done.1, ...), custom_call_target="tpu_custom_call" | custom-call | bytes 900000000 | tf_op jit(solution)/shard_map/level_front/pallas_call | solution.py:650
  89.7 1.8 collective-permute-start.13
  91.5 1.3 copy-done.2
  92.8 8.7 %coupling.4 = (f32[6,128,128]{2,1,0:T(8,128)S(1)}, f32[6,128,128]{2,1,0:T(8,128)S(1)}, f32[6,128,128]{2,1,0:T(8,128)S(1)}) custom-call(s32[2]{0:T(128)S(1)} %pad_add_fusion.pos_ref, f32[16,72,256]{2,1,0:T(8,128)S(1)} %bitcast.13), custom_call_target="tpu_custom_call" | custom-call | bytes 600000 | tf_op jit(solution)/shard_map/coupling/pallas_call | solution.py:629
  102.2 4.3 %own_child.4.base_ref = f32[10,256,256]{2,1,0:T(8,128)S(1)} custom-call(s32[2]{0:T(128)S(1)} %pad_add_fusion.pos_ref, f32[10,128,128]{2,1,0:T(8,128)S(1)} %get-tuple-element.48.pk_ref.own_pk, s32[14,512]{1,0:T(8,128)S(1)} %copy-done.1), custom_call_target="tpu_custom_call" | custom-call | bytes 600000 | tf_op jit(solution)/shard_map/own_child/pallas_call | solution.py:644
  108.0 1.0 copy-done.7
  109.0 1.0 copy-done.9
  110.0 22.7 %level_front.4 = (f32[64,512]{1,0:T(8,128)S(1)}, f32[10,128,128]{2,1,0:T(8,128)S(1)}) custom-call(s32[2]{0:T(128)S(1)} %pad_add_fusion.pos_ref, f32[10,256,256]{2,1,0:T(8,128)S(1)} %own_child.4.base_ref, f32[10,128,128]{2,1,0:T(8,128)S(1)} %get-tuple-element.48.pk_ref.own_pk, s32[14,512]{1,0:T(8,128)S(1)} %copy-done.1, ...), custom_call_target="tpu_custom_call" | custom-call | bytes 900000000 | tf_op jit(solution)/shard_map/level_front/pallas_call | solution.py:650
  133.4 2.6 %collective-permute-start.17 = (f32[5,128,128]{2,1,0:T(8,128)}, f32[5,128,128]{2,1,0:T(8,128)}, u32[]{:S(2)}, u32[]{:S(2)}) collective-permute-start(f32[5,128,128]{2,1,0:T(8,128)} %constant_dynamic-slice_fusion), channel_id=1, source_target_pairs={{0,16},{16,0},{1,17},{17,1},{2,18},{18,2},{3,19},{19,3},{4,20},{20... | collective-permute-start | bytes 983048 | tf_op jit(solution)/shard_map/ppermute | solution.py:626
  136.0 3.7 %own_child.5.base_ref = f32[10,256,256]{2,1,0:T(8,128)S(1)} custom-call(s32[2]{0:T(128)S(1)} %pad_add_fusion.pos_ref, f32[10,128,128]{2,1,0:T(8,128)S(1)} %get-tuple-element.56.pk_ref.own_pk, s32[14,512]{1,0:T(8,128)S(1)} %copy-done.1), custom_call_target="tpu_custom_call" | custom-call | bytes 600000 | tf_op jit(solution)/shard_map/own_child/pallas_call | solution.py:644
  139.7 6.9 %all-gather.11.cloned.1.call-done = f32[1280,256]{1,0:T(8,128)} async-done(((f32[40,256]{1,0:T(8,128)}), f32[1280,256]{1,0:T(8,128)}) %all-gather.11.cloned.1.call-update) | async-done | bytes 1310736 | tf_op jit(solution)/shard_map/all_gather | solution.py:596
  146.7 1.3 copy-done
  148.0 8.4 %coupling.5 = (f32[4,128,128]{2,1,0:T(8,128)S(1)}, f32[4,128,128]{2,1,0:T(8,128)S(1)}, f32[5,128,128]{2,1,0:T(8,128)S(1)}) custom-call(s32[2]{0:T(128)S(1)} %pad_add_fusion.pos_ref, f32[32,40,256]{2,1,0:T(8,128)S(1)} %bitcast.12), custom_call_target="tpu_custom_call" | custom-call | bytes 600000 | tf_op jit(solution)/shard_map/coupling/pallas_call | solution.py:629
  157.5 1.4 collective-permute-done.14.refs_3_
  159.3 21.3 %level_front.5 = (f32[32,512]{1,0:T(8,128)S(1)}, f32[8,128]{1,0:T(8,128)S(1)}) custom-call(s32[2]{0:T(128)S(1)} %pad_add_fusion.pos_ref, f32[10,256,256]{2,1,0:T(8,128)S(1)} %own_child.5.base_ref, f32[10,128,128]{2,1,0:T(8,128)S(1)} %get-tuple-element.56.pk_ref.own_pk, s32[14,512]{1,0:T(8,128)S(1)} %copy-done.1, ...), custom_call_target="tpu_custom_call" | custom-call | bytes 900000000 | tf_op jit(solution)/shard_map/level_front/pallas_call | solution.py:650
  181.2 1.0 maximum_bitcast_fusion
  (64 shorter events, 9.5 us)
Async XLA Ops:
  7.2 44.4 %all-gather.7.cloned.1.call-start = ((), (), s32[]{:S(2)}) async-start(), calls=%async_computation | async-start | bytes 1253376 | tf_op jit(solution)/shard_map/all_gather | solution.py:596
  8.3 14.9 %collective-permute-start.1 = (f32[256,512]{1,0:T(8,128)S(1)}, f32[256,512]{1,0:T(8,128)S(1)}, u32[]{:S(2)}, u32[]{:S(2)}) collective-permute-start(f32[256,512]{1,0:T(8,128)S(1)} %slice.12.refs_0_), channel_id=1, source_target_pairs={{0,2},{1,3},{2,0},{3,1},{4,6},{5,7},{6,4},{7,5},{8,10},{9,11},{10,... | collective-permute-start | bytes 1572872 | tf_op jit(solution)/shard_map/ppermute | solution.py:557
  11.4 0.9 copy-start.12
  23.2 68.3 %all-gather.9.cloned.1.call-start = ((), (), s32[]{:S(2)}) async-start(), calls=%async_computation.1 | async-start | bytes 1253376 | tf_op jit(solution)/shard_map/all_gather | solution.py:596
  24.0 122.7 %all-gather.11.cloned.1.call-start = ((), (), s32[]{:S(2)}) async-start(), calls=%async_computation.2 | async-start | bytes 1351680 | tf_op jit(solution)/shard_map/all_gather | solution.py:596
  24.0 2.0 %collective-permute-start.2 = (f32[256,512]{1,0:T(8,128)S(1)}, f32[256,512]{1,0:T(8,128)S(1)}, u32[]{:S(2)}, u32[]{:S(2)}) collective-permute-start(f32[256,512]{1,0:T(8,128)S(1)} %collective-permute-done.1.refs_2_), channel_id=1, source_target_pairs={{0,1},{1,0},{2,3},{3,2},{4,5},{5,4},{6,7},{7,6},{8,9},{9,8},{10,11... | collective-permute-start | bytes 1572872 | tf_op jit(solution)/shard_map/ppermute | solution.py:557
  24.1 4.5 %collective-permute-start = (f32[256,512]{1,0:T(8,128)S(1)}, f32[256,512]{1,0:T(8,128)S(1)}, u32[]{:S(2)}, u32[]{:S(2)}) collective-permute-start(f32[256,512]{1,0:T(8,128)S(1)} %slice.12.refs_0_), channel_id=1, source_target_pairs={{0,1},{1,0},{2,3},{3,2},{4,5},{5,4},{6,7},{7,6},{8,9},{9,8},{10,11... | collective-permute-start | bytes 1572872 | tf_op jit(solution)/shard_map/ppermute | solution.py:557
  27.1 17.4 %collective-permute-start.4 = (f32[256,512]{1,0:T(8,128)S(1)}, f32[256,512]{1,0:T(8,128)S(1)}, u32[]{:S(2)}, u32[]{:S(2)}) collective-permute-start(f32[256,512]{1,0:T(8,128)S(1)} %slice.10.refs_0_), channel_id=1, source_target_pairs={{2,0},{3,1},{6,4},{7,5},{10,8},{11,9},{14,12},{15,13},{18,16},{19,... | collective-permute-start | bytes 1572872 | tf_op jit(solution)/shard_map/ppermute | solution.py:592
  28.4 19.4 %collective-permute-start.3 = (f32[256,512]{1,0:T(8,128)S(1)}, f32[256,512]{1,0:T(8,128)S(1)}, u32[]{:S(2)}, u32[]{:S(2)}) collective-permute-start(f32[256,512]{1,0:T(8,128)S(1)} %slice.10.refs_0_), channel_id=1, source_target_pairs={{0,1},{1,0},{2,3},{3,2},{4,5},{5,4},{6,7},{7,6},{8,9},{9,8},{10,11... | collective-permute-start | bytes 1572872 | tf_op jit(solution)/shard_map/ppermute | solution.py:557
  44.4 3.3 %collective-permute-start.5 = (f32[256,512]{1,0:T(8,128)S(1)}, f32[256,512]{1,0:T(8,128)S(1)}, u32[]{:S(2)}, u32[]{:S(2)}) collective-permute-start(f32[256,512]{1,0:T(8,128)S(1)} %collective-permute-done.4.refs_2_), channel_id=1, source_target_pairs={{0,1},{1,0},{2,3},{3,2},{4,5},{5,4},{6,7},{7,6},{8,9},{9,8},{10,11... | collective-permute-start | bytes 1572872 | tf_op jit(solution)/shard_map/ppermute | solution.py:557
  47.7 2.0 %copy-start.4 = (f32[256,512]{1,0:T(8,128)}, f32[256,512]{1,0:T(8,128)S(1)}, u32[]{:S(2)}) copy-start(f32[256,512]{1,0:T(8,128)S(1)} %get-tuple-element.36) | copy-start | bytes 1572868
  47.8 14.6 %copy-start.1 = (s32[14,512]{1,0:T(8,128)S(1)}, s32[14,512]{1,0:T(8,128)}, u32[]{:S(2)}) copy-start(s32[14,512]{1,0:T(8,128)} %maps_ref.11) | copy-start | bytes 86020
  49.8 17.1 %collective-permute-start.9 = (f32[10,128,128]{2,1,0:T(8,128)S(1)}, f32[10,128,128]{2,1,0:T(8,128)S(1)}, u32[]{:S(2)}, u32[]{:S(2)}) collective-permute-start(f32[10,128,128]{2,1,0:T(8,128)S(1)} %leaf_update.1.pk_ref.own_pk), channel_id=1, source_target_pairs={{0,4},{4,0},{1,5},{5,1},{2,6},{6,2},{3,7},{7,3},{8,12},{12,8},{9,1... | collective-permute-start | bytes 1966088 | tf_op jit(solution)/shard_map/ppermute | solution.py:623
  51.6 1.2 copy-start.3
  61.7 5.1 %collective-permute-start.6 = (f32[6,128,128]{2,1,0:T(8,128)S(1)}, f32[6,128,128]{2,1,0:T(8,128)S(1)}, u32[]{:S(2)}, u32[]{:S(2)}) collective-permute-start(f32[6,128,128]{2,1,0:T(8,128)S(1)} %get-tuple-element.44.refs_0_), channel_id=1, source_target_pairs={{0,1},{1,0},{2,3},{3,2},{4,5},{5,4},{6,7},{7,6},{8,9},{9,8},{10,11... | collective-permute-start | bytes 1179656 | tf_op jit(solution)/shard_map/ppermute | solution.py:557
  61.8 5.0 %collective-permute-start.7 = (f32[6,128,128]{2,1,0:T(8,128)S(1)}, f32[6,128,128]{2,1,0:T(8,128)S(1)}, u32[]{:S(2)}, u32[]{:S(2)}) collective-permute-start(f32[6,128,128]{2,1,0:T(8,128)S(1)} %get-tuple-element.45.refs_1_), channel_id=1, source_target_pairs={{0,1},{1,0},{2,3},{3,2},{4,5},{5,4},{6,7},{7,6},{8,9},{9,8},{10,11... | collective-permute-start | bytes 1179656 | tf_op jit(solution)/shard_map/ppermute | solution.py:557
  62.3 4.6 %collective-permute-start.8 = (f32[6,128,128]{2,1,0:T(8,128)S(1)}, f32[6,128,128]{2,1,0:T(8,128)S(1)}, u32[]{:S(2)}, u32[]{:S(2)}) collective-permute-start(f32[6,128,128]{2,1,0:T(8,128)S(1)} %get-tuple-element.46.refs_2_), channel_id=1, source_target_pairs={{0,1},{1,0},{2,3},{3,2},{4,5},{5,4},{6,7},{7,6},{8,9},{9,8},{10,11... | collective-permute-start | bytes 1179656 | tf_op jit(solution)/shard_map/ppermute | solution.py:557
  89.7 18.3 %collective-permute-start.13 = (f32[10,128,128]{2,1,0:T(8,128)S(1)}, f32[10,128,128]{2,1,0:T(8,128)S(1)}, u32[]{:S(2)}, u32[]{:S(2)}) collective-permute-start(f32[10,128,128]{2,1,0:T(8,128)S(1)} %get-tuple-element.48.pk_ref.own_pk), channel_id=1, source_target_pairs={{0,8},{8,0},{1,9},{9,1},{2,10},{10,2},{3,11},{11,3},{4,12},{12,4},... | collective-permute-start | bytes 1966088 | tf_op jit(solution)/shard_map/ppermute | solution.py:623
  91.5 1.3 copy-start.2
  101.5 5.0 %collective-permute-start.10 = (f32[6,128,128]{2,1,0:T(8,128)S(1)}, f32[6,128,128]{2,1,0:T(8,128)S(1)}, u32[]{:S(2)}, u32[]{:S(2)}) collective-permute-start(f32[6,128,128]{2,1,0:T(8,128)S(1)} %get-tuple-element.52.refs_0_), channel_id=1, source_target_pairs={{0,1},{1,0},{2,3},{3,2},{4,5},{5,4},{6,7},{7,6},{8,9},{9,8},{10,11... | collective-permute-start | bytes 1179656 | tf_op jit(solution)/shard_map/ppermute | solution.py:557
  101.6 5.7 %collective-permute-start.11 = (f32[6,128,128]{2,1,0:T(8,128)S(1)}, f32[6,128,128]{2,1,0:T(8,128)S(1)}, u32[]{:S(2)}, u32[]{:S(2)}) collective-permute-start(f32[6,128,128]{2,1,0:T(8,128)S(1)} %get-tuple-element.53.refs_1_), channel_id=1, source_target_pairs={{0,1},{1,0},{2,3},{3,2},{4,5},{5,4},{6,7},{7,6},{8,9},{9,8},{10,11... | collective-permute-start | bytes 1179656 | tf_op jit(solution)/shard_map/ppermute | solution.py:557
  102.1 5.9 %collective-permute-start.12 = (f32[6,128,128]{2,1,0:T(8,128)S(1)}, f32[6,128,128]{2,1,0:T(8,128)}, u32[]{:S(2)}, u32[]{:S(2)}) collective-permute-start(f32[6,128,128]{2,1,0:T(8,128)S(1)} %get-tuple-element.54.refs_2_), channel_id=1, source_target_pairs={{0,1},{1,0},{2,3},{3,2},{4,5},{5,4},{6,7},{7,6},{8,9},{9,8},{10,11... | collective-permute-start | bytes 1179656 | tf_op jit(solution)/shard_map/ppermute | solution.py:557
  108.0 1.0 copy-start.7
  109.0 1.0 copy-start.9
  133.4 23.3 %collective-permute-start.17 = (f32[5,128,128]{2,1,0:T(8,128)}, f32[5,128,128]{2,1,0:T(8,128)}, u32[]{:S(2)}, u32[]{:S(2)}) collective-permute-start(f32[5,128,128]{2,1,0:T(8,128)} %constant_dynamic-slice_fusion), channel_id=1, source_target_pairs={{0,16},{16,0},{1,17},{17,1},{2,18},{18,2},{3,19},{19,3},{4,20},{20... | collective-permute-start | bytes 983048 | tf_op jit(solution)/shard_map/ppermute | solution.py:626
  146.6 1.3 copy-start
  156.4 2.9 %collective-permute-start.16 = (f32[5,128,128]{2,1,0:T(8,128)S(1)}, f32[5,128,128]{2,1,0:T(8,128)S(1)}, u32[]{:S(2)}, u32[]{:S(2)}) collective-permute-start(f32[5,128,128]{2,1,0:T(8,128)S(1)} %get-tuple-element.62.refs_2_), channel_id=1, source_target_pairs={{0,1},{1,0},{2,3},{3,2},{4,5},{5,4},{6,7},{7,6},{8,9},{9,8},{10,11... | collective-permute-start | bytes 983048 | tf_op jit(solution)/shard_map/ppermute | solution.py:557
  156.7 2.6 %collective-permute-start.18 = (f32[5,128,128]{2,1,0:T(8,128)}, f32[5,128,128]{2,1,0:T(8,128)S(1)}, u32[]{:S(2)}, u32[]{:S(2)}) collective-permute-start(f32[5,128,128]{2,1,0:T(8,128)} %collective-permute-done.17.refs_6_), channel_id=1, source_target_pairs={{0,1},{1,0},{2,3},{3,2},{4,5},{5,4},{6,7},{7,6},{8,9},{9,8},{10,11... | collective-permute-start | bytes 983048 | tf_op jit(solution)/shard_map/ppermute | solution.py:557
  157.0 2.0 %collective-permute-start.14 = (f32[4,128,128]{2,1,0:T(8,128)S(1)}, f32[4,128,128]{2,1,0:T(8,128)S(1)}, u32[]{:S(2)}, u32[]{:S(2)}) collective-permute-start(f32[4,128,128]{2,1,0:T(8,128)S(1)} %get-tuple-element.60.refs_0_), channel_id=1, source_target_pairs={{0,1},{1,0},{2,3},{3,2},{4,5},{5,4},{6,7},{7,6},{8,9},{9,8},{10,11... | collective-permute-start | bytes 786440 | tf_op jit(solution)/shard_map/ppermute | solution.py:557
  157.2 23.9 %copy-start.5 = (f32[256,512]{1,0:T(8,128)S(1)}, f32[256,512]{1,0:T(8,128)}, u32[]{:S(2)}) copy-start(f32[256,512]{1,0:T(8,128)} %copy-done.4) | copy-start | bytes 1572868
  157.2 23.9 %copy-start.11 = (f32[128,512]{1,0:T(8,128)S(1)}, f32[128,512]{1,0:T(8,128)}, u32[]{:S(2)}) copy-start(f32[128,512]{1,0:T(8,128)} %copy-done.10) | copy-start | bytes 786436
  157.2 2.1 %collective-permute-start.15 = (f32[4,128,128]{2,1,0:T(8,128)S(1)}, f32[4,128,128]{2,1,0:T(8,128)S(1)}, u32[]{:S(2)}, u32[]{:S(2)}) collective-permute-start(f32[4,128,128]{2,1,0:T(8,128)S(1)} %get-tuple-element.61.refs_1_), channel_id=1, source_target_pairs={{0,1},{1,0},{2,3},{3,2},{4,5},{5,4},{6,7},{7,6},{8,9},{9,8},{10,11... | collective-permute-start | bytes 786440 | tf_op jit(solution)/shard_map/ppermute | solution.py:557
  (5 other events, 3.8 us)
Sparse Core Ops, SparseCore 0:
  23.4 26.9 all-gather.6
  52.0 30.8 all-gather.8
  85.7 60.8 all-gather.10
